TPU v7x, 512 devices: a whole 4x4x16 slice. The times are simulated.
512 devices in a mesh: ctx: 128 (over z, y, core), head: 4 (over x).
Axes of the slice: x: 4, y: 4, z: 16, core: 2. Of those that a mesh axis runs over, the one named last changes fastest.
Arguments:
- queries: bfloat16 [16384, 4096], P(('ctx', 'head')), may hold values from -24 to 24
- key_rows: bfloat16 [16384, 4096], P(('ctx', 'head')), may hold values from -12 to 12
- value_rows: bfloat16 [16384, 4096], P(('ctx', 'head')), may hold values from -6 to 6
- rel_bias: float32 [32, 32], P(None, 'head'), may hold values from -4 to 4
- offsets: int32 [2, 32], P(None, 'head'), may hold values from 0 to 63, as said below
Outputs:
- attended: bfloat16 [16384, 4096], P(('ctx', 'head'))
Inputs may be any that keep to these rules, and one draw needn't show every extreme that they name: offsets[0, h] is below 4 and offsets[1, h] is below 64.
All inputs are finite; a program needn't handle non-finite values.
Results may differ from a plain program's by a relative error of at most 0.005.
Values may be sent and summed in bfloat16 or wider, within the bound.
No kernel may reach another device: no remote copies, remote signals or barrier semaphores. Data moves between devices by JAX's collectives and lax.ppermute only.
A program may use at most 64 MiB of HBM per device.

v0:
```python
import math
import jax
import jax.numpy as jnp
from jax import lax
from jax.sharding import PartitionSpec as P

DH = 128
BUCKETS = 32
MAXDIST = 128
R1 = 4
SPAN = 256


def shifted(block, axis, distance):
    devices = range(lax.axis_size(axis))
    route = [(i - distance, i) for i in devices if i - distance in devices]
    return lax.ppermute(block, axis, route)


def bucket_edges():
    half_count = BUCKETS // 2
    thresholds = []
    for target in range(half_count + 1, BUCKETS):
        thresholds.append(
            int(
                math.ceil(
                    half_count * (MAXDIST / half_count) ** ((target - half_count) / half_count)
                )
            )
        )
    return thresholds


def bucket_of(token_separation):
    half_count = BUCKETS // 2
    far_bucket = jnp.full(token_separation.shape, half_count, jnp.int32)
    for border in bucket_edges():
        far_bucket = far_bucket + (token_separation >= border).astype(jnp.int32)
    return jnp.where(token_separation < half_count, token_separation, far_bucket)


def bias_block(position_bias_lookup, ask_count, key_count, advance, stride):
    ask_spots = jnp.arange(ask_count, dtype=jnp.int32)[:, None]
    key_spots = jnp.arange(key_count, dtype=jnp.int32)[None, :]
    token_separation = jnp.maximum((ask_spots - key_spots + advance) * stride, 0)
    bucket_grid = bucket_of(token_separation)
    indicator_matrix = (
        jnp.arange(BUCKETS, dtype=jnp.int32)[:, None, None] == bucket_grid[None]
    ).astype(jnp.float32)
    return jnp.einsum(
        "lnd,lc->cnd", indicator_matrix, position_bias_lookup, precision=lax.Precision.HIGHEST
    )


def start_state(ask_count, n_heads):
    return (
        jnp.full((n_heads, ask_count), -1e30, jnp.float32),
        jnp.zeros((n_heads, ask_count), jnp.float32),
        jnp.zeros((ask_count, n_heads, DH), jnp.float32),
    )


def attend(running, asks, key_part, value_part, advance, stride, position_bias_lookup, usable):
    ask_count = asks.shape[0]
    key_count = key_part.shape[0]
    scores = jnp.einsum(
        "qhd,khd->hqk", asks, key_part, preferred_element_type=jnp.float32
    ) * asks.shape[2] ** (-0.5)
    scores = scores + bias_block(position_bias_lookup, ask_count, key_count, advance, stride)
    allowed = (
        jnp.arange(ask_count, dtype=jnp.int32)[:, None] + advance
        >= jnp.arange(key_count, dtype=jnp.int32)[None, :]
    ) & usable
    held = jnp.where(allowed[None], scores, -1e30)
    row_top, row_sum, row_acc = running
    fresh = jnp.maximum(row_top, jnp.max(held, axis=2))
    weights = jnp.where(allowed[None], jnp.exp(held - fresh[:, :, None]), 0.0)
    shrink = jnp.exp(row_top - fresh)
    row_sum = row_sum * shrink + jnp.sum(weights, axis=2)
    blended = jnp.einsum(
        "hqk,khd->qhd", weights.astype(jnp.bfloat16), value_part, preferred_element_type=jnp.float32
    )
    row_acc = row_acc * jnp.transpose(shrink)[:, :, None] + blended
    return (fresh, row_sum, row_acc)


def finish(running):
    row_top, row_sum, row_acc = running
    result = (row_acc / jnp.transpose(row_sum)[:, :, None]).astype(jnp.bfloat16)
    return (result, jnp.transpose(row_top + jnp.log(row_sum)))


def select_rows(tokens, picks, stride):
    n_rows, n_heads, head_dim = tokens.shape
    grouped = tokens.reshape(n_rows // stride, stride, n_heads, head_dim)
    wanted = jnp.arange(stride, dtype=jnp.int32)[None, :, None, None] == picks[None, None, :, None]
    picked = jnp.where(wanted, grouped, jnp.zeros((), tokens.dtype))
    return jnp.sum(picked, axis=1, dtype=tokens.dtype)


def merge_block(
    first_out, leading_logsumexp, mid_out, mid_lse, far_out, far_lse, mid_pick, far_pick
):
    long_rate = first_out.shape[1]
    spots = jnp.arange(long_rate, dtype=jnp.int32)[:, None]
    mid_cover = (spots % R1 == mid_pick[None, :])[None]
    far_cover = (spots == far_pick[None, :])[None]
    mid_lse_wide = jnp.repeat(mid_lse, R1, axis=1)
    mid_out_wide = jnp.repeat(mid_out, R1, axis=1)
    far_lse_wide = jnp.broadcast_to(far_lse[:, None, :], leading_logsumexp.shape)
    peak = jnp.maximum(
        leading_logsumexp,
        jnp.maximum(
            jnp.where(mid_cover, mid_lse_wide, leading_logsumexp),
            jnp.where(far_cover, far_lse_wide, leading_logsumexp),
        ),
    )
    first_weight = jnp.exp(leading_logsumexp - peak)
    mid_weight = jnp.where(mid_cover, jnp.exp(jnp.where(mid_cover, mid_lse_wide, peak) - peak), 0.0)
    far_weight = jnp.where(far_cover, jnp.exp(jnp.where(far_cover, far_lse_wide, peak) - peak), 0.0)
    blended = (
        first_weight[..., None] * first_out.astype(jnp.float32)
        + mid_weight[..., None] * mid_out_wide.astype(jnp.float32)
        + far_weight[..., None] * far_out[:, None].astype(jnp.float32)
    )
    return (blended / (first_weight + mid_weight + far_weight)[..., None]).astype(jnp.bfloat16)


def nearby_dilation_period(running, asks, moving, kept, position_bias_lookup, position, group):
    tok_rows = asks.shape[0]

    def near_turn(turn_no, carried):
        current_state_value, moving_now, kept_now = carried
        moving_now = shifted(moving_now, "ctx", 1)
        current_state_value = attend(
            current_state_value,
            asks,
            moving_now[0],
            moving_now[1],
            turn_no * tok_rows,
            1,
            position_bias_lookup,
            position >= turn_no,
        )
        return (current_state_value, moving_now, kept_now)

    result = lax.fori_loop(1, group, near_turn, (running, moving, kept))
    return (result[0], result[2])


def mid_cycle(running, asks, moving, position_bias_lookup, position, from_turn, group):
    mid_rows = asks.shape[0]

    def mid_turn(turn_no, carried):
        current_state_value, moving_now = carried
        moving_now = shifted(moving_now, "ctx", 1)
        current_state_value = attend(
            current_state_value,
            asks,
            moving_now[0],
            moving_now[1],
            turn_no * mid_rows,
            R1,
            position_bias_lookup,
            position >= turn_no,
        )
        return (current_state_value, moving_now)

    return lax.fori_loop(from_turn, group, mid_turn, (running, moving))[0]


def on_device(queries, key_rows, value_rows, rel_bias, offsets):
    local_q, local_k, local_v = (
        lax.all_to_all(queries, "head", split_axis=1, concat_axis=0, tiled=True),
        lax.all_to_all(key_rows, "head", split_axis=1, concat_axis=0, tiled=True),
        lax.all_to_all(value_rows, "head", split_axis=1, concat_axis=0, tiled=True),
    )
    tok_rows = local_q.shape[0]
    n_heads = rel_bias.shape[1]
    asks = local_q.reshape(tok_rows, n_heads, DH)
    keys_here = local_k.reshape(tok_rows, n_heads, DH)
    vals_here = local_v.reshape(tok_rows, n_heads, DH)
    n_ctx = lax.axis_size("ctx")
    place = lax.axis_index("ctx")
    long_rate = tok_rows * n_ctx // SPAN
    near_group = SPAN // tok_rows
    mid_rows = tok_rows // R1
    mid_group = R1 * SPAN // tok_rows
    far_rows = tok_rows // long_rate
    mid_pick = offsets[0]
    far_pick = offsets[1]
    mid_q = select_rows(asks, mid_pick, R1)
    mid_k = select_rows(keys_here, mid_pick, R1)
    mid_v = select_rows(vals_here, mid_pick, R1)
    mid_pair = jnp.stack([mid_k, mid_v])
    first_state = attend(
        start_state(tok_rows, n_heads), asks, keys_here, vals_here, 0, 1, rel_bias, True
    )
    first_state, kept = nearby_dilation_period(
        first_state,
        asks,
        jnp.stack([keys_here, vals_here]),
        mid_pair,
        rel_bias,
        place % near_group,
        near_group,
    )
    mid_state = attend(start_state(mid_rows, n_heads), mid_q, mid_k, mid_v, 0, R1, rel_bias, True)
    mid_state = mid_cycle(mid_state, mid_q, mid_pair, rel_bias, place % mid_group, 1, mid_group)
    far_q = select_rows(asks, far_pick, long_rate)
    far_k = select_rows(keys_here, far_pick, long_rate)
    far_v = select_rows(vals_here, far_pick, long_rate)
    far_state = attend(
        start_state(far_rows, n_heads),
        far_q,
        lax.all_gather(far_k, "ctx", axis=0, tiled=True),
        lax.all_gather(far_v, "ctx", axis=0, tiled=True),
        place * far_rows,
        long_rate,
        rel_bias,
        True,
    )
    far_out, far_lse = finish(far_state)
    first_out, leading_logsumexp = finish(first_state)
    mid_out, mid_lse = finish(mid_state)
    merged = merge_block(
        first_out.reshape(far_rows, long_rate, n_heads, DH),
        leading_logsumexp.reshape(far_rows, long_rate, n_heads),
        mid_out.reshape(far_rows, long_rate // R1, n_heads, DH),
        mid_lse.reshape(far_rows, long_rate // R1, n_heads),
        far_out,
        far_lse,
        mid_pick,
        far_pick,
    )
    merged = merged.reshape(tok_rows, n_heads * DH)
    return lax.all_to_all(merged, "head", split_axis=0, concat_axis=1, tiled=True)


def solution(mesh):
    in_specs = (
        P(("ctx", "head"), None),
        P(("ctx", "head"), None),
        P(("ctx", "head"), None),
        P(None, "head"),
        P(None, "head"),
    )
    out_specs = P(("ctx", "head"), None)
    return jax.shard_map(
        on_device, mesh=mesh, in_specs=in_specs, out_specs=out_specs, check_vma=False
    )
```

profile of v0, /device:TPU:128, one launch (start us, length us, event | category | flops | bytes accessed | tf_op | source)
XLA Modules:
  0.0 295.4 jit_solution(1167431653436418967)
XLA Ops:
  0.0 1.7 copy.297
  1.7 4.3 %all-to-all-start = ((bf16[32,4,1024]{2,0,1:T(8,128)(2,1)}), bf16[32,4,1024]{2,0,1:T(8,128)(2,1)S(1)}, u32[]{:S(2)}, u32[]{:S(2)}) async-start(bf16[32,4,1024]{2,0,1:T(8,128)(2,1)} %bitcast.228), calls=%async_computation | async-start | bytes 524288 | tf_op jit(solution)/shard_map/all_to_all | solution.py:174
  6.5 0.3 fusion.53
  7.3 0.7 copy.296
  8.0 0.7 copy.295
  8.7 0.7 fusion.31
  9.4 0.2 copy.204
  9.7 0.7 fusion.30
  10.4 0.2 copy.199
  10.7 2.0 all-to-all-done
  12.7 3.4 %all-to-all-start.1 = ((bf16[32,4,1024]{2,0,1:T(8,128)(2,1)}), bf16[32,4,1024]{2,0,1:T(8,128)(2,1)S(1)}, u32[]{:S(2)}, u32[]{:S(2)}) async-start(bf16[32,4,1024]{2,0,1:T(8,128)(2,1)} %bitcast.227), calls=%async_computation.1 | async-start | bytes 524288 | tf_op jit(solution)/shard_map/all_to_all | solution.py:175
  16.1 6.6 %all-to-all-done.1 = bf16[32,4,1024]{2,0,1:T(8,128)(2,1)S(1)} async-done(((bf16[32,4,1024]{2,0,1:T(8,128)(2,1)}), bf16[32,4,1024]{2,0,1:T(8,128)(2,1)S(1)}, u32[]{:S(2)}, u32[]{:S(2)}) %all-to-all-start.1) | async-done | bytes 262176 | tf_op jit(solution)/shard_map/all_to_all | solution.py:175
  22.7 3.4 %all-to-all-start.2 = ((bf16[32,4,1024]{2,0,1:T(8,128)(2,1)}), bf16[32,4,1024]{2,0,1:T(8,128)(2,1)S(1)}, u32[]{:S(2)}, u32[]{:S(2)}) async-start(bf16[32,4,1024]{2,0,1:T(8,128)(2,1)} %bitcast.226), calls=%async_computation.2 | async-start | bytes 524288 | tf_op jit(solution)/shard_map/all_to_all | solution.py:176
  26.3 6.5 %all-to-all-done.2 = bf16[32,4,1024]{2,0,1:T(8,128)(2,1)S(1)} async-done(((bf16[32,4,1024]{2,0,1:T(8,128)(2,1)}), bf16[32,4,1024]{2,0,1:T(8,128)(2,1)S(1)}, u32[]{:S(2)}, u32[]{:S(2)}) %all-to-all-start.2) | async-done | bytes 262176 | tf_op jit(solution)/shard_map/all_to_all | solution.py:176
  32.8 0.2 fusion.60
  33.2 0.3 select_reduce_fusion
  33.8 0.2 fusion.43
  34.1 85.1 %all_gather.6 = bf16[256,8,128]{2,1,0:T(8,128)(2,1)S(1)} all-gather(bf16[2,8,128]{2,1,0:T(8,128)(2,1)S(1)} %reduce_sum.144), channel_id=1, replica_groups=mesh['ctx'=128,'head'=4] {'ctx'}, dimensions={0}, use_global_device_ids=true | all-gather | bytes 528384 | tf_op jit(solution)/shard_map/all_gather | solution.py:216
  119.2 0.3 fusion.180
  119.7 80.7 %all_gather.7 = bf16[256,8,128]{2,1,0:T(8,128)(2,1)S(1)} all-gather(bf16[2,8,128]{2,1,0:T(8,128)(2,1)S(1)} %reduce_sum.149), channel_id=1, replica_groups=mesh['ctx'=128,'head'=4] {'ctx'}, dimensions={0}, use_global_device_ids=true | all-gather | bytes 528384 | tf_op jit(solution)/shard_map/all_gather | solution.py:217
  200.4 0.2 fusion.50
  200.7 2.4 collective-permute-start.1
  203.2 74.2 %while.4 = (s32[]{:T(128)}, f32[8,32]{1,0:T(8,128)S(1)}, f32[8,32]{1,0:T(8,128)S(1)}, f32[32,8,128]{2,0,1:T(8,128)S(1)}, bf16[2,32,8,128]{3,1,2,0:T(8,128)(2,1)S...) while((s32[]{:T(128)}, f32[8,32]{1,0:T(8,128)S(1)}, ...), condition=%wide.region_12.13_spmd, body=%wide.region_9.12_spmd.sunk | while | flops 7575332 | bytes 1713579 | solution.py:169
  203.2 2.6 collective-permute-start
  205.9 0.3 fusion.194
  206.3 9.7 %collective-permute-done = bf16[2,32,8,128]{3,1,2,0:T(8,128)(2,1)S(1)} collective-permute-done((bf16[2,32,8,128]{3,1,2,0:T(8,128)(2,1)S(1)}, bf16[2,32,8,128]{3,1,2,0:T(8,128)(2,1)S(1)}, u32[]{:S(2)}, u32[]{:S(2)}) %collective-permute-start) | collective-permute-done | bytes 131104 | tf_op jit(solution)/shard_map/while/body/eval_jaxpr/ppermute | solution.py:17
  216.3 0.2 fusion.199
  216.5 1.9 collective-permute-start
  218.5 0.3 fusion.194
  218.9 7.2 %collective-permute-done = bf16[2,32,8,128]{3,1,2,0:T(8,128)(2,1)S(1)} collective-permute-done((bf16[2,32,8,128]{3,1,2,0:T(8,128)(2,1)S(1)}, bf16[2,32,8,128]{3,1,2,0:T(8,128)(2,1)S(1)}, u32[]{:S(2)}, u32[]{:S(2)}) %collective-permute-start) | collective-permute-done | bytes 131104 | tf_op jit(solution)/shard_map/while/body/eval_jaxpr/ppermute | solution.py:17
  226.4 0.2 fusion.199
  226.7 1.9 collective-permute-start
  228.6 0.3 fusion.194
  229.0 7.2 %collective-permute-done = bf16[2,32,8,128]{3,1,2,0:T(8,128)(2,1)S(1)} collective-permute-done((bf16[2,32,8,128]{3,1,2,0:T(8,128)(2,1)S(1)}, bf16[2,32,8,128]{3,1,2,0:T(8,128)(2,1)S(1)}, u32[]{:S(2)}, u32[]{:S(2)}) %collective-permute-start) | collective-permute-done | bytes 131104 | tf_op jit(solution)/shard_map/while/body/eval_jaxpr/ppermute | solution.py:17
  236.5 0.2 fusion.199
  236.8 1.9 collective-permute-start
  238.8 0.3 fusion.194
  239.2 7.2 %collective-permute-done = bf16[2,32,8,128]{3,1,2,0:T(8,128)(2,1)S(1)} collective-permute-done((bf16[2,32,8,128]{3,1,2,0:T(8,128)(2,1)S(1)}, bf16[2,32,8,128]{3,1,2,0:T(8,128)(2,1)S(1)}, u32[]{:S(2)}, u32[]{:S(2)}) %collective-permute-start) | collective-permute-done | bytes 131104 | tf_op jit(solution)/shard_map/while/body/eval_jaxpr/ppermute | solution.py:17
  246.7 0.2 fusion.199
  246.9 1.9 collective-permute-start
  248.9 0.3 fusion.194
  249.3 7.2 %collective-permute-done = bf16[2,32,8,128]{3,1,2,0:T(8,128)(2,1)S(1)} collective-permute-done((bf16[2,32,8,128]{3,1,2,0:T(8,128)(2,1)S(1)}, bf16[2,32,8,128]{3,1,2,0:T(8,128)(2,1)S(1)}, u32[]{:S(2)}, u32[]{:S(2)}) %collective-permute-start) | collective-permute-done | bytes 131104 | tf_op jit(solution)/shard_map/while/body/eval_jaxpr/ppermute | solution.py:17
  256.8 0.2 fusion.199
  257.1 1.9 collective-permute-start
  259.1 0.3 fusion.194
  259.5 7.2 %collective-permute-done = bf16[2,32,8,128]{3,1,2,0:T(8,128)(2,1)S(1)} collective-permute-done((bf16[2,32,8,128]{3,1,2,0:T(8,128)(2,1)S(1)}, bf16[2,32,8,128]{3,1,2,0:T(8,128)(2,1)S(1)}, u32[]{:S(2)}, u32[]{:S(2)}) %collective-permute-start) | collective-permute-done | bytes 131104 | tf_op jit(solution)/shard_map/while/body/eval_jaxpr/ppermute | solution.py:17
  267.0 0.2 fusion.199
  267.2 1.9 collective-permute-start
  269.2 0.3 fusion.194
  269.6 7.2 %collective-permute-done = bf16[2,32,8,128]{3,1,2,0:T(8,128)(2,1)S(1)} collective-permute-done((bf16[2,32,8,128]{3,1,2,0:T(8,128)(2,1)S(1)}, bf16[2,32,8,128]{3,1,2,0:T(8,128)(2,1)S(1)}, u32[]{:S(2)}, u32[]{:S(2)}) %collective-permute-start) | collective-permute-done | bytes 131104 | tf_op jit(solution)/shard_map/while/body/eval_jaxpr/ppermute | solution.py:17
  277.1 0.2 fusion.199
  278.1 0.3 fusion.179
  278.4 1.3 fusion.178
  279.7 0.2 fusion.55
  279.9 0.5 fusion.33
  280.4 1.3 fusion.42
  281.7 0.3 copy.223
  282.3 0.2 div.42
  282.6 0.2 mul.189
  282.9 0.2 mul.183
  283.4 0.9 mul.193
  284.3 1.3 divide_convert_fusion
  285.6 9.1 %all_to_all.64 = bf16[4,32,1024]{2,1,0:T(8,128)(2,1)S(1)} all-to-all(bf16[4,32,1024]{2,1,0:T(8,128)(2,1)S(1)} %divide_convert_fusion), channel_id=1, replica_groups=mesh['ctx'=128,'head'=4] {'head'}, dimensions={0} | all-to-all | bytes 524288 | tf_op jit(solution)/shard_map/all_to_all | solution.py:237
  294.7 0.7 copy.240
  (141 shorter events, 6.0 us)
Async XLA Ops:
  0.0 6.3 %copy-start.3 = (s32[2,8]{1,0:T(2,128)S(1)}, s32[2,8]{1,0:T(2,128)}, u32[]{:S(2)}) copy-start(s32[2,8]{1,0:T(2,128)} %param.11) | copy-start | bytes 196
  0.0 6.3 %copy-start = (f32[32,8]{0,1:T(8,128)S(1)}, f32[32,8]{0,1:T(8,128)}, u32[]{:S(2)}) copy-start(f32[32,8]{0,1:T(8,128)} %param.10) | copy-start | bytes 3076
  1.7 11.0 %all-to-all-start = ((bf16[32,4,1024]{2,0,1:T(8,128)(2,1)}), bf16[32,4,1024]{2,0,1:T(8,128)(2,1)S(1)}, u32[]{:S(2)}, u32[]{:S(2)}) async-start(bf16[32,4,1024]{2,0,1:T(8,128)(2,1)} %bitcast.228), calls=%async_computation | async-start | bytes 524288 | tf_op jit(solution)/shard_map/all_to_all | solution.py:174
  6.0 1.3 copy-start.1
  6.9 1.1 copy-start.2
  12.7 10.1 %all-to-all-start.1 = ((bf16[32,4,1024]{2,0,1:T(8,128)(2,1)}), bf16[32,4,1024]{2,0,1:T(8,128)(2,1)S(1)}, u32[]{:S(2)}, u32[]{:S(2)}) async-start(bf16[32,4,1024]{2,0,1:T(8,128)(2,1)} %bitcast.227), calls=%async_computation.1 | async-start | bytes 524288 | tf_op jit(solution)/shard_map/all_to_all | solution.py:175
  22.7 10.1 %all-to-all-start.2 = ((bf16[32,4,1024]{2,0,1:T(8,128)(2,1)}), bf16[32,4,1024]{2,0,1:T(8,128)(2,1)S(1)}, u32[]{:S(2)}, u32[]{:S(2)}) async-start(bf16[32,4,1024]{2,0,1:T(8,128)(2,1)} %bitcast.226), calls=%async_computation.2 | async-start | bytes 524288 | tf_op jit(solution)/shard_map/all_to_all | solution.py:176
  200.7 77.7 %collective-permute-start.1 = (bf16[2,128,8,128]{3,1,2,0:T(8,128)(2,1)S(1)}, bf16[2,128,8,128]{3,1,2,0:T(8,128)(2,1)}, u32[]{:S(2)}, u32[]{:S(2)}) collective-permute-start(bf16[2,128,8,128]{3,1,2,0:T(8,128)(2,1)S(1)} %pad_maximum_fusion), channel_id=1, source_target_pairs={{0,4},{4,8},{8,12},{12,16},{16,20},{20,24},{24,28},{28,32},{32,36}... | collective-permute-start | bytes 1572872 | tf_op jit(solution)/shard_map/while/body/eval_jaxpr/ppermute | solution.py:17
  203.2 12.8 %collective-permute-start = (bf16[2,32,8,128]{3,1,2,0:T(8,128)(2,1)S(1)}, bf16[2,32,8,128]{3,1,2,0:T(8,128)(2,1)S(1)}, u32[]{:S(2)}, u32[]{:S(2)}) collective-permute-start(bf16[2,32,8,128]{3,1,2,0:T(8,128)(2,1)S(1)} %get-tuple-element.334), channel_id=1, source_target_pairs={{0,4},{4,8},{8,12},{12,16},{16,20},{20,24},{24,28},{28,32},{32,36}... | collective-permute-start | bytes 393224 | tf_op jit(solution)/shard_map/while/body/eval_jaxpr/ppermute | solution.py:17
  216.5 9.6 %collective-permute-start = (bf16[2,32,8,128]{3,1,2,0:T(8,128)(2,1)S(1)}, bf16[2,32,8,128]{3,1,2,0:T(8,128)(2,1)S(1)}, u32[]{:S(2)}, u32[]{:S(2)}) collective-permute-start(bf16[2,32,8,128]{3,1,2,0:T(8,128)(2,1)S(1)} %get-tuple-element.334), channel_id=1, source_target_pairs={{0,4},{4,8},{8,12},{12,16},{16,20},{20,24},{24,28},{28,32},{32,36}... | collective-permute-start | bytes 393224 | tf_op jit(solution)/shard_map/while/body/eval_jaxpr/ppermute | solution.py:17
  226.7 9.6 %collective-permute-start = (bf16[2,32,8,128]{3,1,2,0:T(8,128)(2,1)S(1)}, bf16[2,32,8,128]{3,1,2,0:T(8,128)(2,1)S(1)}, u32[]{:S(2)}, u32[]{:S(2)}) collective-permute-start(bf16[2,32,8,128]{3,1,2,0:T(8,128)(2,1)S(1)} %get-tuple-element.334), channel_id=1, source_target_pairs={{0,4},{4,8},{8,12},{12,16},{16,20},{20,24},{24,28},{28,32},{32,36}... | collective-permute-start | bytes 393224 | tf_op jit(solution)/shard_map/while/body/eval_jaxpr/ppermute | solution.py:17
  236.8 9.6 %collective-permute-start = (bf16[2,32,8,128]{3,1,2,0:T(8,128)(2,1)S(1)}, bf16[2,32,8,128]{3,1,2,0:T(8,128)(2,1)S(1)}, u32[]{:S(2)}, u32[]{:S(2)}) collective-permute-start(bf16[2,32,8,128]{3,1,2,0:T(8,128)(2,1)S(1)} %get-tuple-element.334), channel_id=1, source_target_pairs={{0,4},{4,8},{8,12},{12,16},{16,20},{20,24},{24,28},{28,32},{32,36}... | collective-permute-start | bytes 393224 | tf_op jit(solution)/shard_map/while/body/eval_jaxpr/ppermute | solution.py:17
  246.9 9.6 %collective-permute-start = (bf16[2,32,8,128]{3,1,2,0:T(8,128)(2,1)S(1)}, bf16[2,32,8,128]{3,1,2,0:T(8,128)(2,1)S(1)}, u32[]{:S(2)}, u32[]{:S(2)}) collective-permute-start(bf16[2,32,8,128]{3,1,2,0:T(8,128)(2,1)S(1)} %get-tuple-element.334), channel_id=1, source_target_pairs={{0,4},{4,8},{8,12},{12,16},{16,20},{20,24},{24,28},{28,32},{32,36}... | collective-permute-start | bytes 393224 | tf_op jit(solution)/shard_map/while/body/eval_jaxpr/ppermute | solution.py:17
  257.1 9.6 %collective-permute-start = (bf16[2,32,8,128]{3,1,2,0:T(8,128)(2,1)S(1)}, bf16[2,32,8,128]{3,1,2,0:T(8,128)(2,1)S(1)}, u32[]{:S(2)}, u32[]{:S(2)}) collective-permute-start(bf16[2,32,8,128]{3,1,2,0:T(8,128)(2,1)S(1)} %get-tuple-element.334), channel_id=1, source_target_pairs={{0,4},{4,8},{8,12},{12,16},{16,20},{20,24},{24,28},{28,32},{32,36}... | collective-permute-start | bytes 393224 | tf_op jit(solution)/shard_map/while/body/eval_jaxpr/ppermute | solution.py:17
  267.2 9.6 %collective-permute-start = (bf16[2,32,8,128]{3,1,2,0:T(8,128)(2,1)S(1)}, bf16[2,32,8,128]{3,1,2,0:T(8,128)(2,1)S(1)}, u32[]{:S(2)}, u32[]{:S(2)}) collective-permute-start(bf16[2,32,8,128]{3,1,2,0:T(8,128)(2,1)S(1)} %get-tuple-element.334), channel_id=1, source_target_pairs={{0,4},{4,8},{8,12},{12,16},{16,20},{20,24},{24,28},{28,32},{32,36}... | collective-permute-start | bytes 393224 | tf_op jit(solution)/shard_map/while/body/eval_jaxpr/ppermute | solution.py:17
where the time goes:
time: 296 us; the launch traced here: 295 us
  blocking collectives  175 us (59%)
  waiting for transfers between devices  68 us (23%)
  starting transfers between devices  27.7 us (9%)
  matrix products  10.9 us (4%)
  local copies, waits for them, and re-layouts  8.66 us (3%)
  other arithmetic  4 us (1%)
    all_gather x1, blocking collectives, on_device(): lax.all_gather(far_k, 'ctx', axis=0, tiled=True)  85.1 us
    all_gather x1, blocking collectives, on_device(): lax.all_gather(far_v, 'ctx', axis=0, tiled=True)  80.7 us
    ppermute x8, waiting for transfers between devices, shifted(): return lax.ppermute(block, axis, route)  53 us
    ppermute x8, starting transfers between devices, shifted(): return lax.ppermute(block, axis, route)  16.6 us
    all_to_all x1, blocking collectives, on_device(): lax.all_to_all(merged, 'head', split_axis=0, concat_axis=1, tiled=True)  9.07 us
    all_to_all x1, waiting for transfers between devices, on_device(): lax.all_to_all(key_rows, 'head', split_axis=1, concat_axis=0, tiled=True)  6.57 us
    all_to_all x1, waiting for transfers between devices, on_device(): lax.all_to_all(value_rows, 'head', split_axis=1, concat_axis=0, tiled=True)  6.48 us
  transfers between devices with their start and end apart: 11, of which 10 were waited for; matrix products, arithmetic and copies ran while one was open for 4% of the time, Pallas kernels for 0%

commit v1 on v0

--- a/solution.py
+++ b/solution.py
@@ -214,7 +214,9 @@
         start_state(far_rows, n_heads),
         far_q,
         lax.all_gather(far_k, "ctx", axis=0, tiled=True),
-        lax.all_gather(far_v, "ctx", axis=0, tiled=True),
+        jnp.concatenate(
+            lax.all_to_all(jnp.stack([far_v] * lax.axis_size("ctx")), "ctx", 0, 0), axis=0
+        ),
         place * far_rows,
         long_rate,
         rel_bias,

time: 296 us -> 248 us (0.84)
  blocking collectives: 175 us -> 94.2 us
  waiting for transfers between devices: 68 us -> 83.2 us
  starting transfers between devices: 27.7 us -> 42.1 us
  local copies, waits for them, and re-layouts: 8.66 us -> 11.7 us
    all_gather x1 -> x0, blocking collectives: 80.7 us -> none  [on_device(): lax.all_gather(far_v, 'ctx', axis=0, tiled=True)]
    ppermute x8, waiting for transfers between devices: 53 us -> 68.1 us  [shifted(): return lax.ppermute(block, axis, route)]
    all_to_all x0 -> x1, starting transfers between devices: none -> 13.8 us  [on_device(): lax.all_to_all(jnp.stack([far_v] * lax.axis_size('ctx')), 'ctx', 0, 0)]
  transfers between devices with their start and end apart: 11 -> 12, of which waited for: 10 -> 10; matrix products, arithmetic and copies ran while one was open for 4% -> 8% of each run, Pallas kernels for 0% -> 0%
where the time goes in v1:
time: 248 us; the launch traced here: 247 us
  blocking collectives  94.2 us (38%)
  waiting for transfers between devices  83.2 us (34%)
  starting transfers between devices  42.1 us (17%)
  local copies, waits for them, and re-layouts  11.7 us (5%)
  matrix products  10.9 us (4%)
  other arithmetic  3.79 us (2%)
    all_gather x1, blocking collectives, on_device(): lax.all_gather(far_k, 'ctx', axis=0, tiled=True)  85.1 us
    ppermute x8, waiting for transfers between devices, shifted(): return lax.ppermute(block, axis, route)  68.1 us
    ppermute x8, starting transfers between devices, shifted(): return lax.ppermute(block, axis, route)  17.1 us
    all_to_all x1, starting transfers between devices, on_device(): lax.all_to_all(jnp.stack([far_v] * lax.axis_size('ctx')), 'ctx', 0, 0)  13.8 us
    all_to_all x1, blocking collectives, on_device(): lax.all_to_all(merged, 'head', split_axis=0, concat_axis=1, tiled=True)  9.07 us
    all_to_all x1, waiting for transfers between devices, on_device(): lax.all_to_all(value_rows, 'head', split_axis=1, concat_axis=0, tiled=True)  6.63 us
    all_to_all x1, waiting for transfers between devices, on_device(): lax.all_to_all(key_rows, 'head', split_axis=1, concat_axis=0, tiled=True)  6.57 us
  transfers between devices with their start and end apart: 12, of which 10 were waited for; matrix products, arithmetic and copies ran while one was open for 8% of the time, Pallas kernels for 0%

profile of v1, /device:TPU:128, one launch (start us, length us, event | category | flops | bytes accessed | tf_op | source)
XLA Modules:
  0.0 247.1 jit_solution(13583375859164731686)
XLA Ops:
  0.0 1.7 copy.298
  1.7 4.4 %all-to-all-start = ((bf16[32,4,1024]{2,0,1:T(8,128)(2,1)}), bf16[32,4,1024]{2,0,1:T(8,128)(2,1)S(1)}, u32[]{:S(2)}, u32[]{:S(2)}) async-start(bf16[32,4,1024]{2,0,1:T(8,128)(2,1)} %bitcast.230), calls=%async_computation | async-start | bytes 524288 | tf_op jit(solution)/shard_map/all_to_all | solution.py:174
  6.9 0.7 copy.297
  7.6 0.7 copy.296
  8.4 0.7 fusion.31
  9.4 0.7 fusion.30
  10.2 0.2 copy.201
  10.4 0.3 fusion.51
  10.8 2.0 all-to-all-done
  12.8 3.4 %all-to-all-start.1 = ((bf16[32,4,1024]{2,0,1:T(8,128)(2,1)}), bf16[32,4,1024]{2,0,1:T(8,128)(2,1)S(1)}, u32[]{:S(2)}, u32[]{:S(2)}) async-start(bf16[32,4,1024]{2,0,1:T(8,128)(2,1)} %bitcast.229), calls=%async_computation.1 | async-start | bytes 524288 | tf_op jit(solution)/shard_map/all_to_all | solution.py:175
  16.3 6.6 %all-to-all-done.1 = bf16[32,4,1024]{2,0,1:T(8,128)(2,1)S(1)} async-done(((bf16[32,4,1024]{2,0,1:T(8,128)(2,1)}), bf16[32,4,1024]{2,0,1:T(8,128)(2,1)S(1)}, u32[]{:S(2)}, u32[]{:S(2)}) %all-to-all-start.1) | async-done | bytes 262176 | tf_op jit(solution)/shard_map/all_to_all | solution.py:175
  22.8 3.4 %all-to-all-start.2 = ((bf16[32,4,1024]{2,0,1:T(8,128)(2,1)}), bf16[32,4,1024]{2,0,1:T(8,128)(2,1)S(1)}, u32[]{:S(2)}, u32[]{:S(2)}) async-start(bf16[32,4,1024]{2,0,1:T(8,128)(2,1)} %bitcast.228), calls=%async_computation.2 | async-start | bytes 524288 | tf_op jit(solution)/shard_map/all_to_all | solution.py:176
  26.3 6.6 %all-to-all-done.2 = bf16[32,4,1024]{2,0,1:T(8,128)(2,1)S(1)} async-done(((bf16[32,4,1024]{2,0,1:T(8,128)(2,1)}), bf16[32,4,1024]{2,0,1:T(8,128)(2,1)S(1)}, u32[]{:S(2)}, u32[]{:S(2)}) %all-to-all-start.2) | async-done | bytes 262176 | tf_op jit(solution)/shard_map/all_to_all | solution.py:176
  32.9 0.2 fusion.58
  33.2 85.1 %all_gather.3 = bf16[256,8,128]{2,1,0:T(8,128)(2,1)S(1)} all-gather(bf16[2,8,128]{2,1,0:T(8,128)(2,1)S(1)} %reduce_sum.144), channel_id=1, replica_groups=mesh['ctx'=128,'head'=4] {'ctx'}, dimensions={0}, use_global_device_ids=true | all-gather | bytes 528384 | tf_op jit(solution)/shard_map/all_gather | solution.py:216
  118.3 0.3 fusion.179
  119.0 1.1 stack.14
  120.1 13.8 %all-to-all-start.3 = ((bf16[128,2,8,128]{3,1,2,0:T(2,128)(2,1)}), bf16[128,2,8,128]{3,1,2,0:T(2,128)(2,1)S(1)}, u32[]{:S(2)}, u32[]{:S(2)}) async-start(bf16[128,2,8,128]{3,1,2,0:T(2,128)(2,1)} %stack.14), calls=%async_computation.3 | async-start | bytes 1048576 | tf_op jit(solution)/shard_map/all_to_all | solution.py:218
  134.1 0.9 pad_maximum_fusion
  134.9 2.2 collective-permute-start.1
  137.2 0.3 select_reduce_fusion
  138.1 90.0 %while.4 = (s32[]{:T(128)}, f32[8,32]{1,0:T(8,128)S(1)}, f32[8,32]{1,0:T(8,128)S(1)}, f32[32,8,128]{2,0,1:T(8,128)S(1)}, bf16[2,32,8,128]{3,1,2,0:T(8,128)(2,1)S...) while((s32[]{:T(128)}, f32[8,32]{1,0:T(8,128)S(1)}, ...), condition=%wide.region_12.13_spmd, body=%wide.region_9.12_spmd.sunk | while | flops 7575332 | bytes 1713579 | solution.py:169
  138.1 3.4 %collective-permute-start = (bf16[2,32,8,128]{3,1,2,0:T(8,128)(2,1)S(1)}, bf16[2,32,8,128]{3,1,2,0:T(8,128)(2,1)S(1)}, u32[]{:S(2)}, u32[]{:S(2)}) collective-permute-start(bf16[2,32,8,128]{3,1,2,0:T(8,128)(2,1)S(1)} %get-tuple-element.334), channel_id=1, source_target_pairs={{0,4},{4,8},{8,12},{12,16},{16,20},{20,24},{24,28},{28,32},{32,36}... | collective-permute-start | bytes 393224 | tf_op jit(solution)/shard_map/while/body/eval_jaxpr/ppermute | solution.py:17
  141.5 0.3 fusion.194
  141.9 24.7 %collective-permute-done = bf16[2,32,8,128]{3,1,2,0:T(8,128)(2,1)S(1)} collective-permute-done((bf16[2,32,8,128]{3,1,2,0:T(8,128)(2,1)S(1)}, bf16[2,32,8,128]{3,1,2,0:T(8,128)(2,1)S(1)}, u32[]{:S(2)}, u32[]{:S(2)}) %collective-permute-start) | collective-permute-done | bytes 131104 | tf_op jit(solution)/shard_map/while/body/eval_jaxpr/ppermute | solution.py:17
  166.9 0.2 fusion.199
  167.2 1.9 collective-permute-start
  169.2 0.3 fusion.194
  169.6 7.2 %collective-permute-done = bf16[2,32,8,128]{3,1,2,0:T(8,128)(2,1)S(1)} collective-permute-done((bf16[2,32,8,128]{3,1,2,0:T(8,128)(2,1)S(1)}, bf16[2,32,8,128]{3,1,2,0:T(8,128)(2,1)S(1)}, u32[]{:S(2)}, u32[]{:S(2)}) %collective-permute-start) | collective-permute-done | bytes 131104 | tf_op jit(solution)/shard_map/while/body/eval_jaxpr/ppermute | solution.py:17
  177.1 0.2 fusion.199
  177.3 1.9 collective-permute-start
  179.3 0.3 fusion.194
  179.7 7.2 %collective-permute-done = bf16[2,32,8,128]{3,1,2,0:T(8,128)(2,1)S(1)} collective-permute-done((bf16[2,32,8,128]{3,1,2,0:T(8,128)(2,1)S(1)}, bf16[2,32,8,128]{3,1,2,0:T(8,128)(2,1)S(1)}, u32[]{:S(2)}, u32[]{:S(2)}) %collective-permute-start) | collective-permute-done | bytes 131104 | tf_op jit(solution)/shard_map/while/body/eval_jaxpr/ppermute | solution.py:17
  187.2 0.2 fusion.199
  187.5 1.9 collective-permute-start
  189.5 0.3 fusion.194
  189.9 7.2 %collective-permute-done = bf16[2,32,8,128]{3,1,2,0:T(8,128)(2,1)S(1)} collective-permute-done((bf16[2,32,8,128]{3,1,2,0:T(8,128)(2,1)S(1)}, bf16[2,32,8,128]{3,1,2,0:T(8,128)(2,1)S(1)}, u32[]{:S(2)}, u32[]{:S(2)}) %collective-permute-start) | collective-permute-done | bytes 131104 | tf_op jit(solution)/shard_map/while/body/eval_jaxpr/ppermute | solution.py:17
  197.4 0.2 fusion.199
  197.6 1.9 collective-permute-start
  199.6 0.3 fusion.194
  200.0 7.2 %collective-permute-done = bf16[2,32,8,128]{3,1,2,0:T(8,128)(2,1)S(1)} collective-permute-done((bf16[2,32,8,128]{3,1,2,0:T(8,128)(2,1)S(1)}, bf16[2,32,8,128]{3,1,2,0:T(8,128)(2,1)S(1)}, u32[]{:S(2)}, u32[]{:S(2)}) %collective-permute-start) | collective-permute-done | bytes 131104 | tf_op jit(solution)/shard_map/while/body/eval_jaxpr/ppermute | solution.py:17
  207.5 0.2 fusion.199
  207.8 1.9 collective-permute-start
  209.7 0.3 fusion.194
  210.1 7.2 %collective-permute-done = bf16[2,32,8,128]{3,1,2,0:T(8,128)(2,1)S(1)} collective-permute-done((bf16[2,32,8,128]{3,1,2,0:T(8,128)(2,1)S(1)}, bf16[2,32,8,128]{3,1,2,0:T(8,128)(2,1)S(1)}, u32[]{:S(2)}, u32[]{:S(2)}) %collective-permute-start) | collective-permute-done | bytes 131104 | tf_op jit(solution)/shard_map/while/body/eval_jaxpr/ppermute | solution.py:17
  217.7 0.2 fusion.199
  217.9 1.9 collective-permute-start
  219.9 0.3 fusion.194
  220.3 7.2 %collective-permute-done = bf16[2,32,8,128]{3,1,2,0:T(8,128)(2,1)S(1)} collective-permute-done((bf16[2,32,8,128]{3,1,2,0:T(8,128)(2,1)S(1)}, bf16[2,32,8,128]{3,1,2,0:T(8,128)(2,1)S(1)}, u32[]{:S(2)}, u32[]{:S(2)}) %collective-permute-start) | collective-permute-done | bytes 131104 | tf_op jit(solution)/shard_map/while/body/eval_jaxpr/ppermute | solution.py:17
  227.8 0.2 fusion.199
  228.5 0.3 fusion.178
  228.8 1.3 fusion.177
  230.4 0.5 fusion.33
  230.8 1.3 fusion.42
  232.1 0.3 copy.225
  233.5 0.9 mul.190
  234.6 0.9 mul.193
  235.5 0.4 copy.229
  235.9 0.3 copy-done.6
  236.2 0.2 fusion.135
  236.6 0.4 copy-done
  237.0 0.3 divide_convert_fusion
  237.3 9.1 %all_to_all.69 = bf16[4,32,1024]{2,1,0:T(8,128)(2,1)S(1)} all-to-all(bf16[4,32,1024]{2,1,0:T(8,128)(2,1)S(1)} %divide_convert_fusion), channel_id=1, replica_groups=mesh['ctx'=128,'head'=4] {'head'}, dimensions={0} | all-to-all | bytes 524288 | tf_op jit(solution)/shard_map/all_to_all | solution.py:239
  246.4 0.7 copy.243
  (157 shorter events, 7.1 us)
Async XLA Ops:
  0.0 6.4 %copy-start.9 = (s32[2,8]{1,0:T(2,128)S(1)}, s32[2,8]{1,0:T(2,128)}, u32[]{:S(2)}) copy-start(s32[2,8]{1,0:T(2,128)} %param.11) | copy-start | bytes 196
  1.7 5.2 %copy-start.3 = (bf16[32,4096]{1,0:T(8,128)(2,1)S(1)}, bf16[32,4096]{1,0:T(8,128)(2,1)}, u32[]{:S(2)}) copy-start(bf16[32,4096]{1,0:T(8,128)(2,1)} %param.8) | copy-start | bytes 786436
  1.7 11.1 %all-to-all-start = ((bf16[32,4,1024]{2,0,1:T(8,128)(2,1)}), bf16[32,4,1024]{2,0,1:T(8,128)(2,1)S(1)}, u32[]{:S(2)}, u32[]{:S(2)}) async-start(bf16[32,4,1024]{2,0,1:T(8,128)(2,1)} %bitcast.230), calls=%async_computation | async-start | bytes 524288 | tf_op jit(solution)/shard_map/all_to_all | solution.py:174
  6.3 1.3 copy-start.4
  6.8 1.4 copy-start.2
  12.8 10.1 %all-to-all-start.1 = ((bf16[32,4,1024]{2,0,1:T(8,128)(2,1)}), bf16[32,4,1024]{2,0,1:T(8,128)(2,1)S(1)}, u32[]{:S(2)}, u32[]{:S(2)}) async-start(bf16[32,4,1024]{2,0,1:T(8,128)(2,1)} %bitcast.229), calls=%async_computation.1 | async-start | bytes 524288 | tf_op jit(solution)/shard_map/all_to_all | solution.py:175
  16.3 102.4 %copy-start.7 = (pred[2,256]{1,0:T(4,128)(4,1)}, pred[2,256]{1,0:T(4,128)(4,1)S(1)}, u32[]{:S(2)}) copy-start(pred[2,256]{1,0:T(4,128)(4,1)S(1)} %iota_compare_fusion.15) | copy-start | bytes 1540
  22.8 10.1 %all-to-all-start.2 = ((bf16[32,4,1024]{2,0,1:T(8,128)(2,1)}), bf16[32,4,1024]{2,0,1:T(8,128)(2,1)S(1)}, u32[]{:S(2)}, u32[]{:S(2)}) async-start(bf16[32,4,1024]{2,0,1:T(8,128)(2,1)} %bitcast.228), calls=%async_computation.2 | async-start | bytes 524288 | tf_op jit(solution)/shard_map/all_to_all | solution.py:176
  118.6 1.5 copy-start.5
  120.1 115.4 %all-to-all-start.3 = ((bf16[128,2,8,128]{3,1,2,0:T(2,128)(2,1)}), bf16[128,2,8,128]{3,1,2,0:T(2,128)(2,1)S(1)}, u32[]{:S(2)}, u32[]{:S(2)}) async-start(bf16[128,2,8,128]{3,1,2,0:T(2,128)(2,1)} %stack.14), calls=%async_computation.3 | async-start | bytes 1048576 | tf_op jit(solution)/shard_map/all_to_all | solution.py:218
  134.9 93.9 %collective-permute-start.1 = (bf16[2,128,8,128]{3,1,2,0:T(8,128)(2,1)}, bf16[2,128,8,128]{3,1,2,0:T(8,128)(2,1)}, u32[]{:S(2)}, u32[]{:S(2)}) collective-permute-start(bf16[2,128,8,128]{3,1,2,0:T(8,128)(2,1)} %pad_maximum_fusion), channel_id=1, source_target_pairs={{0,4},{4,8},{8,12},{12,16},{16,20},{20,24},{24,28},{28,32},{32,36}... | collective-permute-start | bytes 1572872 | tf_op jit(solution)/shard_map/while/body/eval_jaxpr/ppermute | solution.py:17
  138.1 28.6 %collective-permute-start = (bf16[2,32,8,128]{3,1,2,0:T(8,128)(2,1)S(1)}, bf16[2,32,8,128]{3,1,2,0:T(8,128)(2,1)S(1)}, u32[]{:S(2)}, u32[]{:S(2)}) collective-permute-start(bf16[2,32,8,128]{3,1,2,0:T(8,128)(2,1)S(1)} %get-tuple-element.334), channel_id=1, source_target_pairs={{0,4},{4,8},{8,12},{12,16},{16,20},{20,24},{24,28},{28,32},{32,36}... | collective-permute-start | bytes 393224 | tf_op jit(solution)/shard_map/while/body/eval_jaxpr/ppermute | solution.py:17
  167.2 9.6 %collective-permute-start = (bf16[2,32,8,128]{3,1,2,0:T(8,128)(2,1)S(1)}, bf16[2,32,8,128]{3,1,2,0:T(8,128)(2,1)S(1)}, u32[]{:S(2)}, u32[]{:S(2)}) collective-permute-start(bf16[2,32,8,128]{3,1,2,0:T(8,128)(2,1)S(1)} %get-tuple-element.334), channel_id=1, source_target_pairs={{0,4},{4,8},{8,12},{12,16},{16,20},{20,24},{24,28},{28,32},{32,36}... | collective-permute-start | bytes 393224 | tf_op jit(solution)/shard_map/while/body/eval_jaxpr/ppermute | solution.py:17
  177.3 9.6 %collective-permute-start = (bf16[2,32,8,128]{3,1,2,0:T(8,128)(2,1)S(1)}, bf16[2,32,8,128]{3,1,2,0:T(8,128)(2,1)S(1)}, u32[]{:S(2)}, u32[]{:S(2)}) collective-permute-start(bf16[2,32,8,128]{3,1,2,0:T(8,128)(2,1)S(1)} %get-tuple-element.334), channel_id=1, source_target_pairs={{0,4},{4,8},{8,12},{12,16},{16,20},{20,24},{24,28},{28,32},{32,36}... | collective-permute-start | bytes 393224 | tf_op jit(solution)/shard_map/while/body/eval_jaxpr/ppermute | solution.py:17
  187.5 9.6 %collective-permute-start = (bf16[2,32,8,128]{3,1,2,0:T(8,128)(2,1)S(1)}, bf16[2,32,8,128]{3,1,2,0:T(8,128)(2,1)S(1)}, u32[]{:S(2)}, u32[]{:S(2)}) collective-permute-start(bf16[2,32,8,128]{3,1,2,0:T(8,128)(2,1)S(1)} %get-tuple-element.334), channel_id=1, source_target_pairs={{0,4},{4,8},{8,12},{12,16},{16,20},{20,24},{24,28},{28,32},{32,36}... | collective-permute-start | bytes 393224 | tf_op jit(solution)/shard_map/while/body/eval_jaxpr/ppermute | solution.py:17
  197.6 9.6 %collective-permute-start = (bf16[2,32,8,128]{3,1,2,0:T(8,128)(2,1)S(1)}, bf16[2,32,8,128]{3,1,2,0:T(8,128)(2,1)S(1)}, u32[]{:S(2)}, u32[]{:S(2)}) collective-permute-start(bf16[2,32,8,128]{3,1,2,0:T(8,128)(2,1)S(1)} %get-tuple-element.334), channel_id=1, source_target_pairs={{0,4},{4,8},{8,12},{12,16},{16,20},{20,24},{24,28},{28,32},{32,36}... | collective-permute-start | bytes 393224 | tf_op jit(solution)/shard_map/while/body/eval_jaxpr/ppermute | solution.py:17
  207.8 9.6 %collective-permute-start = (bf16[2,32,8,128]{3,1,2,0:T(8,128)(2,1)S(1)}, bf16[2,32,8,128]{3,1,2,0:T(8,128)(2,1)S(1)}, u32[]{:S(2)}, u32[]{:S(2)}) collective-permute-start(bf16[2,32,8,128]{3,1,2,0:T(8,128)(2,1)S(1)} %get-tuple-element.334), channel_id=1, source_target_pairs={{0,4},{4,8},{8,12},{12,16},{16,20},{20,24},{24,28},{28,32},{32,36}... | collective-permute-start | bytes 393224 | tf_op jit(solution)/shard_map/while/body/eval_jaxpr/ppermute | solution.py:17
  217.9 9.6 %collective-permute-start = (bf16[2,32,8,128]{3,1,2,0:T(8,128)(2,1)S(1)}, bf16[2,32,8,128]{3,1,2,0:T(8,128)(2,1)S(1)}, u32[]{:S(2)}, u32[]{:S(2)}) collective-permute-start(bf16[2,32,8,128]{3,1,2,0:T(8,128)(2,1)S(1)} %get-tuple-element.334), channel_id=1, source_target_pairs={{0,4},{4,8},{8,12},{12,16},{16,20},{20,24},{24,28},{28,32},{32,36}... | collective-permute-start | bytes 393224 | tf_op jit(solution)/shard_map/while/body/eval_jaxpr/ppermute | solution.py:17
  235.5 0.7 copy-start.6
  235.5 0.7 copy-start.8
  235.5 1.1 copy-start.1
  235.9 1.1 copy-start
